TPU v7x, 32 devices: a whole 2x2x4 slice. The times are simulated.
32 devices in a mesh: tm: 8 (over y, x, core), head: 4 (over z).
Axes of the slice: x: 2, y: 2, z: 4, core: 2. Of those that a mesh axis runs over, the one named last changes fastest.
Arguments:
- queries: bfloat16 [4096, 1024], P('tm', 'head'), may hold values from -5.5 to 5.5
- key_states: bfloat16 [4096, 1024], P('tm', 'head'), may hold values from -5.5 to 5.5
- value_states: bfloat16 [4096, 1024], P('tm', 'head'), may hold values from -6 to 6
- out_weight: bfloat16 [1024, 1024], P('head'), may hold values from -6 to 6
- upstream: bfloat16 [4096, 1024], P('tm'), may hold values from -6 to 6
- windows: int32 [16], P('head'), may hold values from 64 to 256, as said below
- offsets: int32 [16], P('head'), may hold values from 0 to 7
Outputs:
- mixed: bfloat16 [4096, 1024], P('tm')
- grad_queries: bfloat16 [4096, 1024], P('tm', 'head')
- grad_keys: bfloat16 [4096, 1024], P('tm', 'head')
- grad_values: bfloat16 [4096, 1024], P('tm', 'head')
Inputs may be any that keep to these rules, and one draw needn't show every extreme that they name: `windows`: each head's window reaches at most 256 positions to each side, and some head's window is exactly 256.
All inputs are finite; a program needn't handle non-finite values.
Results may differ from a plain program's by a relative error of at most 0.017.
Values may be sent and summed in bfloat16 or wider, within the bound.
A program may use at most 128 MiB of HBM per device.

v0:
```python
import functools
import math

import jax
import jax.numpy as jnp
from jax import lax
from jax.experimental import pallas as pl
from jax.experimental.pallas import tpu as pltpu
from jax.sharding import PartitionSpec as P

MESH = pl.DeviceIdType.MESH
F32 = jnp.float32
BF16 = jnp.bfloat16
NEG = -1e30


def nt(a, b):
    return lax.dot_general(a, b, (((1,), (1,)), ((), ())), preferred_element_type=F32)


def nn(a, b):
    return lax.dot_general(a, b, (((1,), (0,)), ((), ())), preferred_element_type=F32)


def flipped(me, x):
    peer = me
    for k in range(x.bit_length()):
        if x >> k & 1:
            peer = peer + (1 - 2 * (me // 2**k % 2)) * 2**k
    return peer


def kernel(
    tm, nz, heads,
    q_ref, k_ref, v_ref, w_ref, up_ref, win_ref, off_ref,
    dq_ref, dk_ref, dv_ref, attn_ref,
    order, back, q4, g4, gt, kvnat, kvown, nkv, pkv, ownt, nt_kv, pt_kv,
    cown, cp1, cp2, top, total, delta, ot, dqt,
    accn, accp, acco, sendn, sendp, gotn, gotp, attng, send_sem, recv_sem,
):
    rows, width = q_ref.shape
    dim = width // heads
    levels = tm.bit_length() - 1
    half = rows // 2
    slab = rows // tm
    quarter = rows // 4
    scale = 1.0 / math.sqrt(dim)
    me = lax.axis_index("tm")
    zi = lax.axis_index("head")
    right = (me + 1) % tm
    left = (me + tm - 1) % tm

    barrier = pltpu.get_barrier_semaphore()
    for x in range(1, tm):
        pl.semaphore_signal(
            barrier, inc=1, device_id=((me + x) % tm, zi), device_id_type=MESH
        )
    for x in range(1, nz):
        pl.semaphore_signal(
            barrier, inc=1, device_id=(me, (zi + x) % nz), device_id_type=MESH
        )

    def count_of(x):
        return rows >> x.bit_length()

    def slot_of(x):
        m = x.bit_length()
        return (m - 1) * half + (x - 2 ** (m - 1)) * (rows >> m)

    def remote(src, dst, sem, device):
        return pltpu.make_async_remote_copy(
            src_ref=src, dst_ref=dst, send_sem=send_sem.at[sem], recv_sem=recv_sem.at[sem],
            device_id=device, device_id_type=MESH,
        )

    kvnat[:, :width] = k_ref[...]
    kvnat[:, width:] = v_ref[...]
    pl.semaphore_wait(barrier, tm + nz - 2)
    near = [
        remote(kvnat.at[pl.ds(half, half)], nkv.at[pl.ds(0, half)], 0, (right, zi)),
        remote(kvnat.at[pl.ds(0, half)], nkv.at[pl.ds(half, half)], 1, (left, zi)),
    ]
    for copy in near:
        copy.start()

    def reversed_bits(s):
        out = jnp.zeros_like(s)
        for k in range(levels):
            out = out + ((s >> k) & 1) * 2 ** (levels - 1 - k)
        return out

    def place(row):
        return (row % slab) * tm + reversed_bits(row // slab)

    iota = lambda shape, axis: lax.broadcasted_iota(jnp.int32, shape, axis)
    place_col = place(iota((rows, 1), 0))
    place_row = place(iota((1, rows), 1))
    order[...] = jnp.where(iota((rows, rows), 1) == place_col, 1.0, 0.0).astype(BF16)
    back[...] = jnp.where(iota((rows, rows), 0) == place_row, 1.0, 0.0).astype(BF16)

    def off_cols(cols):
        head = (iota((1, cols), 1) % width) // dim
        out = jnp.zeros((1, cols), jnp.int32)
        for h in range(heads):
            out = jnp.where(head == h, off_ref[h], out)
        return out

    def swapped(x):
        off = off_cols(x.shape[1])
        for k in range(levels):
            size = slab * 2 ** (levels - 1 - k)
            other = jnp.concatenate(
                [x[(i ^ 1) * size : (i ^ 1) * size + size] for i in range(rows // size)], 0
            )
            x = jnp.where(((off >> k) & 1) == 1, other, x)
        return x

    def to_order(x):
        return swapped(nn(order[...], x))

    def from_order(x):
        return nn(back[...], swapped(x).astype(BF16))

    kvp = to_order(kvnat[...])
    kvown[...] = kvp.astype(BF16)
    far = [
        remote(
            kvown.at[pl.ds(0, count_of(x))], pkv.at[pl.ds(slot_of(x), count_of(x))], 1 + x,
            (flipped(me, x), zi),
        )
        for x in range(1, tm)
    ]
    for copy in far:
        copy.start()
    ownt[...] = jnp.transpose(kvp).astype(BF16)
    col_head = iota((1, width), 1) // dim
    qp = to_order(q_ref[...]) * scale
    grad = nt(up_ref[...], w_ref[...]).astype(BF16)
    gp = to_order(grad)
    gt[...] = jnp.transpose(gp)
    for h in range(heads):
        at = pl.ds(h * rows, rows)
        q4[at, :] = jnp.where(col_head == h, qp, 0.0).astype(BF16)
        g4[at, :] = jnp.where(col_head == h, gp, 0.0).astype(BF16)

    def shared(i, j, first):
        out = jnp.zeros(jnp.broadcast_shapes(i.shape, j.shape), F32)
        for l in range(first, levels + 1):
            out = out + jnp.where(jnp.maximum(i, j) < (rows >> l), 1.0, 0.0)
        return out

    cown[...] = shared(iota((1, rows), 1), iota((rows, 1), 0), 1)
    cp1[...] = shared(iota((1, half), 1), iota((half, 1), 0), 1)
    for m in range(2, levels + 1):
        cp2[pl.ds((m - 2) * half, half), :] = shared(
            iota((1, quarter), 1), iota((half, 1), 0) % (rows >> m), m
        )

    near_row = iota((rows, 1), 0)
    gap = 8 * rows
    pos_near = jnp.where(
        near_row < half,
        jnp.where(me > 0, near_row - half, -gap),
        jnp.where(me < tm - 1, near_row + half, gap),
    )

    def own_count(h):
        off = off_ref[h] % tm
        d = (place_col ^ off) - (place_row ^ off)
        return cown[...] + jnp.where(jnp.abs(d) <= win_ref[h], 1.0, 0.0)

    def near_hit(h):
        off = off_ref[h] % tm
        return jnp.abs(pos_near - (place_row ^ off)) <= win_ref[h]

    def sum0(x):
        return jnp.sum(x, axis=0, keepdims=True)

    def max0(x):
        return jnp.max(x, axis=0, keepdims=True)

    def head_rows(h, count):
        return pl.ds(pl.multiple_of(h * rows, rows), count)

    def feat(h):
        return pl.ds(pl.multiple_of(h * dim, dim), dim)

    def vfeat(h):
        return pl.ds(pl.multiple_of(width + h * dim, dim), dim)

    def own_forward(h, _):
        s = nt(kvown[:, :width], q4[head_rows(h, rows), :])
        c = own_count(h)
        s = jnp.where(c > 0.0, s, NEG)
        m = max0(s)
        p = c * jnp.exp(s - m)
        top[h] = m
        total[h] = sum0(p)
        ot[feat(h), :] = nn(ownt[vfeat(h), :], p.astype(BF16))
        return 0

    lax.fori_loop(0, heads, own_forward, 0)

    for copy in near + far:
        copy.wait()
    nt_kv[...] = jnp.transpose(nkv[...].astype(F32)).astype(BF16)
    pt_kv[...] = jnp.transpose(pkv[...].astype(F32)).astype(BF16)

    def widen(a, fill):
        missing = rows - a.shape[1]
        return jnp.concatenate([a, jnp.full((a.shape[0], missing), fill, F32)], 1)

    def other_forward(h, _):
        sn = nt(nkv[:, :width], q4[head_rows(h, rows), :])
        s1 = nt(pkv[:half, :width], q4[head_rows(h, half), :])
        s2 = nt(pkv[half:, :width], q4[head_rows(h, quarter), :])
        sn = jnp.where(near_hit(h), sn, NEG)
        c2 = cp2[...]
        s2 = jnp.where(c2 > 0.0, s2, NEG)
        m0 = top[h]
        m = jnp.maximum(
            jnp.maximum(m0, max0(sn)),
            jnp.maximum(widen(max0(s1), NEG), widen(max0(s2), NEG)),
        )
        pn = jnp.exp(sn - m)
        p1 = cp1[...] * jnp.exp(s1 - m[:, :half])
        p2 = c2 * jnp.exp(s2 - m[:, :quarter])
        keep = jnp.exp(m0 - m)
        l = total[h] * keep + sum0(pn) + widen(sum0(p1), 0.0) + widen(sum0(p2), 0.0)
        o = ot[feat(h), :] * keep + nn(nt_kv[vfeat(h), :], pn.astype(BF16))
        o = o + widen(nn(pt_kv[vfeat(h), :half], p1.astype(BF16)), 0.0)
        o = o + widen(nn(pt_kv[vfeat(h), half:], p2.astype(BF16)), 0.0)
        o = (o / l).astype(BF16).astype(F32)
        ot[feat(h), :] = o
        top[h] = m + jnp.log(l)
        delta[h] = sum0(o * gt[feat(h), :])
        return 0

    lax.fori_loop(0, heads, other_forward, 0)

    attng[zi] = from_order(jnp.transpose(ot[...])).astype(BF16)
    spread = [
        remote(attng.at[zi], attng.at[zi], 2 * tm + 1 + x, (me, (zi + x) % nz))
        for x in range(1, nz)
    ]
    for copy in spread:
        copy.start()

    accn[...] = jnp.zeros_like(accn)
    accp[...] = jnp.zeros_like(accp)
    acco[...] = jnp.zeros_like(acco)

    def back_part(h, kv, at, kt, queries, s_of, c_of):
        q = q4[head_rows(h, queries), :]
        g = g4[head_rows(h, queries), :]
        s = s_of(nt(kv[at, :width], q))
        p = jnp.exp(s - top[h][:, :queries])
        p = c_of(p)
        dots = nt(kv[at, width:], g)
        ds = (p * (dots - delta[h][:, :queries])).astype(BF16)
        return nn(ds, q), nn(p.astype(BF16), g), nn(kt, ds)

    def other_backward(h, _):
        everything = slice(None)
        dk, dv, dq = back_part(
            h, nkv, everything, nt_kv[feat(h), :], rows,
            lambda s: jnp.where(near_hit(h), s, NEG), lambda p: p,
        )
        accn[:, :width] += dk
        accn[:, width:] += dv
        dk, dv, more = back_part(
            h, pkv, slice(0, half), pt_kv[feat(h), :half], half,
            lambda s: s, lambda p: cp1[...] * p,
        )
        dq = dq + widen(more, 0.0)
        accp[:half, :width] += dk
        accp[:half, width:] += dv
        c2 = cp2[...]
        dk, dv, more = back_part(
            h, pkv, slice(half, None), pt_kv[feat(h), half:], quarter,
            lambda s: jnp.where(c2 > 0.0, s, NEG), lambda p: c2 * p,
        )
        dq = dq + widen(more, 0.0)
        accp[half:, :width] += dk
        accp[half:, width:] += dv
        dqt[feat(h), :] = dq
        return 0

    lax.fori_loop(0, heads, other_backward, 0)
    sendn[...] = accn[...].astype(BF16)
    sendp[...] = accp[...].astype(BF16)
    base = tm + 1
    home = [
        remote(sendn.at[pl.ds(half, half)], gotn.at[pl.ds(0, half)], base, (right, zi)),
        remote(sendn.at[pl.ds(0, half)], gotn.at[pl.ds(half, half)], base + 1, (left, zi)),
    ] + [
        remote(
            sendp.at[pl.ds(slot_of(x), count_of(x))], gotp.at[pl.ds(slot_of(x), count_of(x))],
            base + 1 + x, (flipped(me, x), zi),
        )
        for x in range(1, tm)
    ]
    for copy in home:
        copy.start()

    def own_backward(h, _):
        c = own_count(h)
        dk, dv, dq = back_part(
            h, kvown, slice(None), ownt[feat(h), :], rows,
            lambda s: jnp.where(c > 0.0, s, NEG), lambda p: c * p,
        )
        acco[:, :width] += dk
        acco[:, width:] += dv
        dqt[feat(h), :] += dq
        return 0

    lax.fori_loop(0, heads, own_backward, 0)
    dq_ref[...] = from_order(jnp.transpose(dqt[...]) * scale).astype(BF16)

    for copy in home:
        copy.wait()
    for x in range(1, tm):
        acco[: count_of(x), :] += gotp[slot_of(x) : slot_of(x) + count_of(x), :].astype(F32)
    dkv = from_order(acco[...]) + gotn[...].astype(F32)
    dk_ref[...] = dkv[:, :width].astype(BF16)
    dv_ref[...] = dkv[:, width:].astype(BF16)
    for copy in spread:
        copy.wait()
    for z in range(nz):
        attn_ref[:, z * width : (z + 1) * width] = attng[z]


def on_device(tm, nz, queries, key_states, value_states, out_weight, upstream, windows, offsets):
    rows, width = queries.shape
    heads = windows.shape[0]
    levels = tm.bit_length() - 1
    half, quarter = rows // 2, rows // 4
    peers = levels * half
    vmem = pl.BlockSpec(memory_space=pltpu.VMEM)
    smem = pl.BlockSpec(memory_space=pltpu.SMEM)
    small = jax.ShapeDtypeStruct((rows, width), BF16)
    weight = lax.all_gather(out_weight, "head", axis=0, tiled=True)
    sems = 2 * (tm + 1) + nz
    dq, dk, dv, attn = pl.pallas_call(
        functools.partial(kernel, tm, nz, heads),
        out_shape=(small, small, small, jax.ShapeDtypeStruct((rows, nz * width), BF16)),
        in_specs=[vmem] * 5 + [smem] * 2,
        out_specs=(vmem,) * 4,
        scratch_shapes=[
            pltpu.VMEM((rows, rows), BF16),
            pltpu.VMEM((rows, rows), BF16),
            pltpu.VMEM((heads * rows, width), BF16),
            pltpu.VMEM((heads * rows, width), BF16),
            pltpu.VMEM((width, rows), F32),
            pltpu.VMEM((rows, 2 * width), BF16),
            pltpu.VMEM((rows, 2 * width), BF16),
            pltpu.VMEM((rows, 2 * width), BF16),
            pltpu.VMEM((peers, 2 * width), BF16),
            pltpu.VMEM((2 * width, rows), BF16),
            pltpu.VMEM((2 * width, rows), BF16),
            pltpu.VMEM((2 * width, peers), BF16),
            pltpu.VMEM((rows, rows), F32),
            pltpu.VMEM((half, half), F32),
            pltpu.VMEM((peers - half, quarter), F32),
            pltpu.VMEM((heads, 1, rows), F32),
            pltpu.VMEM((heads, 1, rows), F32),
            pltpu.VMEM((heads, 1, rows), F32),
            pltpu.VMEM((width, rows), F32),
            pltpu.VMEM((width, rows), F32),
            pltpu.VMEM((rows, 2 * width), F32),
            pltpu.VMEM((peers, 2 * width), F32),
            pltpu.VMEM((rows, 2 * width), F32),
            pltpu.VMEM((rows, 2 * width), BF16),
            pltpu.VMEM((peers, 2 * width), BF16),
            pltpu.VMEM((rows, 2 * width), BF16),
            pltpu.VMEM((peers, 2 * width), BF16),
            pltpu.VMEM((nz, rows, width), BF16),
            pltpu.SemaphoreType.DMA((sems,)),
            pltpu.SemaphoreType.DMA((sems,)),
        ],
        compiler_params=pltpu.CompilerParams(
            collective_id=0, has_side_effects=True, vmem_limit_bytes=50 * 2**20
        ),
        cost_estimate=pl.CostEstimate(
            flops=20 * 10**9, bytes_accessed=6 * 2**20, transcendentals=6 * 10**6
        ),
    )(queries, key_states, value_states, out_weight, upstream, windows, offsets)
    mixed = jnp.dot(attn, weight, preferred_element_type=F32).astype(BF16)
    return mixed, dq, dk, dv


def solution(mesh):
    placed = (
        P("tm", "head"),
        P("tm", "head"),
        P("tm", "head"),
        P("head", None),
        P("tm", None),
        P("head"),
        P("head"),
    )
    return jax.shard_map(
        functools.partial(on_device, mesh.shape["tm"], mesh.shape["head"]),
        mesh=mesh,
        in_specs=placed,
        out_specs=(P("tm", None), P("tm", "head"), P("tm", "head"), P("tm", "head")),
        check_vma=False,
    )
```

profile of v0, /device:TPU:15, one launch (start us, length us, event | category | flops | bytes accessed | tf_op | source)
XLA Modules:
  0.0 91.4 jit_solution(3363736602016254953)
XLA Ops:
  7.2 0.0 all-gather.2.cloned.1.call-start
  7.2 0.7 all-gather.2.cloned.1.call-update
  7.9 0.0 copy-start
  7.9 1.0 %copy-done = bf16[256,1024]{1,0:T(8,128)(2,1)S(1)} copy-done((bf16[256,1024]{1,0:T(8,128)(2,1)S(1)}, bf16[256,1024]{1,0:T(8,128)(2,1)}, u32[]{:S(2)}) %copy-start) | copy-done | bytes 524312
  8.9 0.0 copy-start.1
  8.9 0.9 %copy-done.1 = bf16[512,256]{1,0:T(8,128)(2,1)S(1)} copy-done((bf16[512,256]{1,0:T(8,128)(2,1)S(1)}, bf16[512,256]{1,0:T(8,128)(2,1)}, u32[]{:S(2)}) %copy-start.1) | copy-done | bytes 262168
  9.9 0.0 copy-start.2
  9.9 0.9 %copy-done.2 = bf16[512,256]{1,0:T(8,128)(2,1)S(1)} copy-done((bf16[512,256]{1,0:T(8,128)(2,1)S(1)}, bf16[512,256]{1,0:T(8,128)(2,1)}, u32[]{:S(2)}) %copy-start.2) | copy-done | bytes 262168
  10.8 0.0 copy-start.3
  10.8 0.9 %copy-done.3 = bf16[512,256]{1,0:T(8,128)(2,1)S(1)} copy-done((bf16[512,256]{1,0:T(8,128)(2,1)S(1)}, bf16[512,256]{1,0:T(8,128)(2,1)}, u32[]{:S(2)}) %copy-start.3) | copy-done | bytes 262168
  11.8 0.0 copy-start.4
  11.8 0.7 copy-done.4
  12.5 0.0 copy-start.5
  12.5 0.7 copy-done.5
  13.1 65.5 %shard_map.102 = (bf16[512,256]{1,0:T(8,128)(2,1)S(1)}, bf16[512,256]{1,0:T(8,128)(2,1)S(1)}, bf16[512,256]{1,0:T(8,128)(2,1)S(1)}, bf16[512,1024]{1,0:T(8,128)(2,1)S(1)}) custom-call(bf16[512,256]{1,0:T(8,128)(2,1)S(1)} %copy-done.1, bf16[512,256]{1,0:T(8,128)(2,1)S(1)} %copy-done.2, bf16[512,256]{1,0:T(8,128)(2,1)S(1)} %copy-done.3, ...), custom_call_target="tpu_custom_call" | custom-call | flops 20000000000 | bytes 6291456 | tf_op jit(solution)/shard_map/pallas_call | solution.py:344
  78.6 0.0 all-gather.2.cloned.1.call-done
  78.6 3.8 %convolution_convert_fusion = bf16[512,1024]{1,0:T(8,128)(2,1)} fusion(bf16[512,1024]{1,0:T(8,128)(2,1)S(1)} %get-tuple-element.8, bf16[1024,1024]{1,0:T(8,128)(2,1)} %all-gather.2.cloned.1.call-done), kind=kOutput, calls=%fused_computation | convolution fusion | flops 1074266112 | bytes 4194304 | tf_op jit(solution)/shard_map/dot_general | solution.py:388
  82.4 0.7 copy.14
  83.1 0.7 copy.15
  83.8 0.7 copy.16
Async XLA Ops:
  7.2 71.4 %all-gather.2.cloned.1.call-start = ((), (), s32[]{:S(2)}) async-start(), calls=%async_computation | async-start | bytes 2621440 | tf_op jit(solution)/shard_map/all_gather | solution.py:342
  7.9 1.0 %copy-start = (bf16[256,1024]{1,0:T(8,128)(2,1)S(1)}, bf16[256,1024]{1,0:T(8,128)(2,1)}, u32[]{:S(2)}) copy-start(bf16[256,1024]{1,0:T(8,128)(2,1)} %w_ref.1) | copy-start | bytes 1572868
  8.9 0.9 %copy-start.1 = (bf16[512,256]{1,0:T(8,128)(2,1)S(1)}, bf16[512,256]{1,0:T(8,128)(2,1)}, u32[]{:S(2)}) copy-start(bf16[512,256]{1,0:T(8,128)(2,1)} %q_ref.1) | copy-start | bytes 786436
  9.9 0.9 %copy-start.2 = (bf16[512,256]{1,0:T(8,128)(2,1)S(1)}, bf16[512,256]{1,0:T(8,128)(2,1)}, u32[]{:S(2)}) copy-start(bf16[512,256]{1,0:T(8,128)(2,1)} %k_ref.1) | copy-start | bytes 786436
  10.8 0.9 %copy-start.3 = (bf16[512,256]{1,0:T(8,128)(2,1)S(1)}, bf16[512,256]{1,0:T(8,128)(2,1)}, u32[]{:S(2)}) copy-start(bf16[512,256]{1,0:T(8,128)(2,1)} %v_ref.1) | copy-start | bytes 786436
  11.8 0.7 copy-start.4
  12.5 0.7 copy-start.5
Sparse Core Ops, SparseCore 0:
  9.6 62.8 all-gather.1
where the time goes:
time: 91.8 us; the launch traced here: 91.4 us
  Pallas kernels  65.5 us (71%)
  between operations  14.1 us (15%)
  local copies, waits for them, and re-layouts  7.3 us (8%)
  matrix products  3.81 us (4%)
    pallas_call x1, Pallas kernels, on_device(): pl.pallas_call(functools.partial(kernel, tm, nz, heads), out_shape=(small...  65.5 us
    unnamed x15, local copies, waits for them, and re-layouts  7.3 us
    dot_general x1, matrix products, on_device(): mixed = jnp.dot(attn, weight, preferred_element_type=F32).astype(BF16)  3.81 us
  transfers between devices with their start and end apart: 1, of which 0 were waited for; matrix products, arithmetic and copies ran while one was open for 0% of the time, Pallas kernels for 72%

commit v1 on v0

--- a/solution.py
+++ b/solution.py
@@ -32,13 +32,14 @@
 
 def kernel(
     tm, nz, heads,
-    q_ref, k_ref, v_ref, w_ref, up_ref, win_ref, off_ref,
-    dq_ref, dk_ref, dv_ref, attn_ref,
+    q_in, k_in, v_in, w_in, up_in, win_ref, off_ref,
+    mixed_ref, dq_ref, dk_ref, dv_ref,
+    q_ref, up_ref, weights,
     order, back, q4, g4, gt, kvnat, kvown, nkv, pkv, ownt, nt_kv, pt_kv,
     cown, cp1, cp2, top, total, delta, ot, dqt,
-    accn, accp, acco, sendn, sendp, gotn, gotp, attng, send_sem, recv_sem,
+    accn, accp, acco, sendn, sendp, gotn, gotp, attng, load_sem, send_sem, recv_sem,
 ):
-    rows, width = q_ref.shape
+    rows, width = q_in.shape
     dim = width // heads
     levels = tm.bit_length() - 1
     half = rows // 2
@@ -47,6 +48,20 @@
     scale = 1.0 / math.sqrt(dim)
     me = lax.axis_index("tm")
     zi = lax.axis_index("head")
+    loads = [
+        pltpu.make_async_copy(src, dst, load_sem.at[i])
+        for i, (src, dst) in enumerate(
+            [
+                (k_in, kvnat.at[:, pl.ds(0, width)]),
+                (v_in, kvnat.at[:, pl.ds(width, width)]),
+                (w_in, weights.at[zi]),
+                (q_in, q_ref),
+                (up_in, up_ref),
+            ]
+        )
+    ]
+    for load in loads:
+        load.start()
     right = (me + 1) % tm
     left = (me + tm - 1) % tm
 
@@ -73,9 +88,9 @@
             device_id=device, device_id_type=MESH,
         )
 
-    kvnat[:, :width] = k_ref[...]
-    kvnat[:, width:] = v_ref[...]
     pl.semaphore_wait(barrier, tm + nz - 2)
+    loads[0].wait()
+    loads[1].wait()
     near = [
         remote(kvnat.at[pl.ds(half, half)], nkv.at[pl.ds(0, half)], 0, (right, zi)),
         remote(kvnat.at[pl.ds(0, half)], nkv.at[pl.ds(half, half)], 1, (left, zi)),
@@ -121,6 +136,15 @@
     def from_order(x):
         return nn(back[...], swapped(x).astype(BF16))
 
+    part = pl.ds(pl.multiple_of((me % 2) * (width // 2), width // 2), width // 2)
+    loads[2].wait()
+    wide = [
+        remote(
+            weights.at[zi, part], weights.at[zi, part], 2 * tm + 1 + nz + x,
+            (me, (zi + x) % nz),
+        )
+        for x in range(1, nz)
+    ]
     kvp = to_order(kvnat[...])
     kvown[...] = kvp.astype(BF16)
     far = [
@@ -130,12 +154,14 @@
         )
         for x in range(1, tm)
     ]
-    for copy in far:
+    for copy in far + wide:
         copy.start()
+    loads[3].wait()
+    loads[4].wait()
     ownt[...] = jnp.transpose(kvp).astype(BF16)
     col_head = iota((1, width), 1) // dim
     qp = to_order(q_ref[...]) * scale
-    grad = nt(up_ref[...], w_ref[...]).astype(BF16)
+    grad = nt(up_ref[...], weights[zi]).astype(BF16)
     gp = to_order(grad)
     gt[...] = jnp.transpose(gp)
     for h in range(heads):
@@ -287,6 +313,18 @@
         return 0
 
     lax.fori_loop(0, heads, other_backward, 0)
+    for copy in wide:
+        copy.wait()
+    twin = []
+    for x in range(1, nz):
+        z = (zi + nz - x) % nz
+        twin.append(
+            remote(
+                weights.at[z, part], weights.at[z, part], 2 * tm + 1 + 2 * nz + x,
+                (flipped(me, 1), zi),
+            )
+        )
+        twin[-1].start()
     sendn[...] = accn[...].astype(BF16)
     sendp[...] = accp[...].astype(BF16)
     base = tm + 1
@@ -317,6 +355,12 @@
     lax.fori_loop(0, heads, own_backward, 0)
     dq_ref[...] = from_order(jnp.transpose(dqt[...]) * scale).astype(BF16)
 
+    for copy in spread + twin:
+        copy.wait()
+    mixed = nn(attng[0], weights[0])
+    for z in range(1, nz):
+        mixed = mixed + nn(attng[z], weights[z])
+    mixed_ref[...] = mixed.astype(BF16)
     for copy in home:
         copy.wait()
     for x in range(1, tm):
@@ -324,10 +368,6 @@
     dkv = from_order(acco[...]) + gotn[...].astype(F32)
     dk_ref[...] = dkv[:, :width].astype(BF16)
     dv_ref[...] = dkv[:, width:].astype(BF16)
-    for copy in spread:
-        copy.wait()
-    for z in range(nz):
-        attn_ref[:, z * width : (z + 1) * width] = attng[z]
 
 
 def on_device(tm, nz, queries, key_states, value_states, out_weight, upstream, windows, offsets):
@@ -339,14 +379,18 @@
     vmem = pl.BlockSpec(memory_space=pltpu.VMEM)
     smem = pl.BlockSpec(memory_space=pltpu.SMEM)
     small = jax.ShapeDtypeStruct((rows, width), BF16)
-    weight = lax.all_gather(out_weight, "head", axis=0, tiled=True)
-    sems = 2 * (tm + 1) + nz
-    dq, dk, dv, attn = pl.pallas_call(
+    model = out_weight.shape[1]
+    hbm = pl.BlockSpec(memory_space=pltpu.HBM)
+    sems = 2 * (tm + 1) + 3 * nz
+    return pl.pallas_call(
         functools.partial(kernel, tm, nz, heads),
-        out_shape=(small, small, small, jax.ShapeDtypeStruct((rows, nz * width), BF16)),
-        in_specs=[vmem] * 5 + [smem] * 2,
+        out_shape=(jax.ShapeDtypeStruct((rows, model), BF16), small, small, small),
+        in_specs=[hbm] * 5 + [smem] * 2,
         out_specs=(vmem,) * 4,
         scratch_shapes=[
+            pltpu.VMEM((rows, width), BF16),
+            pltpu.VMEM((rows, model), BF16),
+            pltpu.VMEM((nz, width, model), BF16),
             pltpu.VMEM((rows, rows), BF16),
             pltpu.VMEM((rows, rows), BF16),
             pltpu.VMEM((heads * rows, width), BF16),
@@ -375,18 +419,17 @@
             pltpu.VMEM((rows, 2 * width), BF16),
             pltpu.VMEM((peers, 2 * width), BF16),
             pltpu.VMEM((nz, rows, width), BF16),
+            pltpu.SemaphoreType.DMA((5,)),
             pltpu.SemaphoreType.DMA((sems,)),
             pltpu.SemaphoreType.DMA((sems,)),
         ],
         compiler_params=pltpu.CompilerParams(
-            collective_id=0, has_side_effects=True, vmem_limit_bytes=50 * 2**20
+            collective_id=0, has_side_effects=True, vmem_limit_bytes=60 * 2**20
         ),
         cost_estimate=pl.CostEstimate(
             flops=20 * 10**9, bytes_accessed=6 * 2**20, transcendentals=6 * 10**6
         ),
     )(queries, key_states, value_states, out_weight, upstream, windows, offsets)
-    mixed = jnp.dot(attn, weight, preferred_element_type=F32).astype(BF16)
-    return mixed, dq, dk, dv
 
 
 def solution(mesh):

time: 91.8 us -> 63.7 us (0.69)
  between operations: 14.1 us -> 0.65 us
  Pallas kernels: 65.5 us -> 57.8 us
  matrix products: 3.81 us -> 0 us
  local copies, waits for them, and re-layouts: 7.3 us -> 5.1 us
    pallas_call x1, Pallas kernels: 65.5 us -> 57.8 us  [on_device(): pl.pallas_call(functools.partial(kernel, tm, nz, heads), out_shape=(jax.S...]
    dot_general x1 -> x0, matrix products: 3.81 us -> none  [on_device(): mixed = jnp.dot(attn, weight, preferred_element_type=F32).astype(BF16)]
    unnamed x15 -> x10, local copies, waits for them, and re-layouts: 7.3 us -> 5.1 us
  transfers between devices with their start and end apart: 1 -> 0, of which waited for: 0 -> 0; matrix products, arithmetic and copies ran while one was open for 0% -> 0% of each run, Pallas kernels for 72% -> 0%
where the time goes in v1:
time: 63.7 us; the launch traced here: 63.5 us
  Pallas kernels  57.8 us (91%)
  local copies, waits for them, and re-layouts  5.1 us (8%)
  between operations  0.65 us (1%)
    pallas_call x1, Pallas kernels, on_device(): pl.pallas_call(functools.partial(kernel, tm, nz, heads), out_shape=(jax.S...  57.8 us
    unnamed x10, local copies, waits for them, and re-layouts  5.1 us

profile of v1, /device:TPU:15, one launch (start us, length us, event | category | flops | bytes accessed | tf_op | source)
XLA Modules:
  0.0 63.5 jit_solution(5563878905119921727)
XLA Ops:
  0.6 57.8 %shard_map.102 = (bf16[512,1024]{1,0:T(8,128)(2,1)}, bf16[512,256]{1,0:T(8,128)(2,1)}, bf16[512,256]{1,0:T(8,128)(2,1)}, bf16[512,256]{1,0:T(8,128)(2,1)}) custom-call(bf16[512,256]{1,0:T(8,128)(2,1)} %q_in.1, bf16[512,256]{1,0:T(8,128)(2,1)} %k_in.1, bf16[512,256]{1,0:T(8,128)(2,1)} %v_in.1, bf16[256,1024]{1,0:T(8,128)(2,1)} %w_in.1, ...), custom_call_target="tpu_custom_call" | custom-call | flops 20000000000 | bytes 6291456 | tf_op jit(solution)/shard_map/pallas_call | solution.py:385
  58.4 0.0 copy-start.2
  58.4 2.3 %copy.15 = bf16[512,1024]{1,0:T(8,128)(2,1)} copy(bf16[512,1024]{1,0:T(8,128)(2,1)} %get-tuple-element.8) | data formatting | bytes 2097152
  60.7 0.0 copy-done.2
  60.7 0.0 copy-start.1
  60.7 0.7 %copy.16 = bf16[512,256]{1,0:T(8,128)(2,1)} copy(bf16[512,256]{1,0:T(8,128)(2,1)S(1)} %copy-done.2) | data formatting | bytes 524288
  61.4 0.3 copy-done.1
  61.8 0.0 copy-start
  61.8 0.7 %copy.17 = bf16[512,256]{1,0:T(8,128)(2,1)} copy(bf16[512,256]{1,0:T(8,128)(2,1)S(1)} %copy-done.1) | data formatting | bytes 524288
  62.5 0.3 copy-done
  62.8 0.7 %copy.18 = bf16[512,256]{1,0:T(8,128)(2,1)} copy(bf16[512,256]{1,0:T(8,128)(2,1)S(1)} %copy-done) | data formatting | bytes 524288
Async XLA Ops:
  58.4 2.3 %copy-start.2 = (bf16[512,256]{1,0:T(8,128)(2,1)S(1)}, bf16[512,256]{1,0:T(8,128)(2,1)}, u32[]{:S(2)}) copy-start(bf16[512,256]{1,0:T(8,128)(2,1)} %get-tuple-element.9) | copy-start | bytes 786436
  60.7 1.0 %copy-start.1 = (bf16[512,256]{1,0:T(8,128)(2,1)S(1)}, bf16[512,256]{1,0:T(8,128)(2,1)}, u32[]{:S(2)}) copy-start(bf16[512,256]{1,0:T(8,128)(2,1)} %get-tuple-element.10) | copy-start | bytes 786436
  61.8 1.0 %copy-start = (bf16[512,256]{1,0:T(8,128)(2,1)S(1)}, bf16[512,256]{1,0:T(8,128)(2,1)}, u32[]{:S(2)}) copy-start(bf16[512,256]{1,0:T(8,128)(2,1)} %get-tuple-element.11) | copy-start | bytes 786436

commit v2 on v1

--- a/solution.py
+++ b/solution.py
@@ -265,12 +265,27 @@
     lax.fori_loop(0, heads, other_forward, 0)
 
     attng[zi] = from_order(jnp.transpose(ot[...])).astype(BF16)
-    spread = [
-        remote(attng.at[zi], attng.at[zi], 2 * tm + 1 + x, (me, (zi + x) % nz))
-        for x in range(1, nz)
-    ]
-    for copy in spread:
-        copy.start()
+    def hop(step, up):
+        block = (zi - step + 1 + nz) % nz if up else (zi + step - 1) % nz
+        peer = (zi + 1) % nz if up else (zi + nz - 1) % nz
+        sem = 2 * tm + 1 + step + (0 if up else 3 * nz)
+        holds = zi >= step - 1 if up else zi <= nz - step
+        gets = zi >= step if up else zi < nz - step
+        sends = jnp.logical_and(holds, zi < nz - 1 if up else zi > 0)
+        return remote(attng.at[block], attng.at[block], sem, (me, peer)), sends, gets
+
+    def hop_start(step):
+        for up in (True, False):
+            copy, sends, _ = hop(step, up)
+            pl.when(sends)(copy.start)
+
+    def hop_wait(step):
+        for up in (True, False):
+            copy, sends, gets = hop(step, up)
+            pl.when(sends)(copy.wait_send)
+            pl.when(gets)(copy.wait_recv)
+
+    hop_start(1)
 
     accn[...] = jnp.zeros_like(accn)
     accp[...] = jnp.zeros_like(accp)
@@ -313,6 +328,8 @@
         return 0
 
     lax.fori_loop(0, heads, other_backward, 0)
+    hop_wait(1)
+    hop_start(2)
     for copy in wide:
         copy.wait()
     twin = []
@@ -355,7 +372,11 @@
     lax.fori_loop(0, heads, own_backward, 0)
     dq_ref[...] = from_order(jnp.transpose(dqt[...]) * scale).astype(BF16)
 
-    for copy in spread + twin:
+    for step in range(2, nz):
+        hop_wait(step)
+        if step < nz - 1:
+            hop_start(step + 1)
+    for copy in twin:
         copy.wait()
     mixed = nn(attng[0], weights[0])
     for z in range(1, nz):
@@ -381,7 +402,7 @@
     small = jax.ShapeDtypeStruct((rows, width), BF16)
     model = out_weight.shape[1]
     hbm = pl.BlockSpec(memory_space=pltpu.HBM)
-    sems = 2 * (tm + 1) + 3 * nz
+    sems = 2 * (tm + 1) + 4 * nz
     return pl.pallas_call(
         functools.partial(kernel, tm, nz, heads),
         out_shape=(jax.ShapeDtypeStruct((rows, model), BF16), small, small, small),

time: 63.7 us -> 59.6 us (0.936)
  the two profiles are of different devices: /device:TPU:15 before, /device:TPU:0 now
where the time goes in v2:
time: 59.6 us; the launch traced here: 59.4 us
  Pallas kernels  53.7 us (90%)
  local copies, waits for them, and re-layouts  5.1 us (9%)
  between operations  0.65 us (1%)
    pallas_call x1, Pallas kernels, on_device(): pl.pallas_call(functools.partial(kernel, tm, nz, heads), out_shape=(jax.S...  53.7 us
    unnamed x10, local copies, waits for them, and re-layouts  5.1 us

profile of v2, /device:TPU:0, one launch (start us, length us, event | category | flops | bytes accessed | tf_op | source)
XLA Modules:
  0.0 59.4 jit_solution(14703453275221190156)
XLA Ops:
  0.6 53.7 %shard_map.102 = (bf16[512,1024]{1,0:T(8,128)(2,1)}, bf16[512,256]{1,0:T(8,128)(2,1)}, bf16[512,256]{1,0:T(8,128)(2,1)}, bf16[512,256]{1,0:T(8,128)(2,1)}) custom-call(bf16[512,256]{1,0:T(8,128)(2,1)} %q_in.1, bf16[512,256]{1,0:T(8,128)(2,1)} %k_in.1, bf16[512,256]{1,0:T(8,128)(2,1)} %v_in.1, bf16[256,1024]{1,0:T(8,128)(2,1)} %w_in.1, ...), custom_call_target="tpu_custom_call" | custom-call | flops 20000000000 | bytes 6291456 | tf_op jit(solution)/shard_map/pallas_call | solution.py:406
  54.3 0.0 copy-start.2
  54.3 2.3 %copy.15 = bf16[512,1024]{1,0:T(8,128)(2,1)} copy(bf16[512,1024]{1,0:T(8,128)(2,1)} %get-tuple-element.8) | data formatting | bytes 2097152
  56.6 0.0 copy-done.2
  56.6 0.0 copy-start.1
  56.6 0.7 %copy.16 = bf16[512,256]{1,0:T(8,128)(2,1)} copy(bf16[512,256]{1,0:T(8,128)(2,1)S(1)} %copy-done.2) | data formatting | bytes 524288
  57.3 0.3 copy-done.1
  57.7 0.0 copy-start
  57.7 0.7 %copy.17 = bf16[512,256]{1,0:T(8,128)(2,1)} copy(bf16[512,256]{1,0:T(8,128)(2,1)S(1)} %copy-done.1) | data formatting | bytes 524288
  58.4 0.3 copy-done
  58.7 0.7 %copy.18 = bf16[512,256]{1,0:T(8,128)(2,1)} copy(bf16[512,256]{1,0:T(8,128)(2,1)S(1)} %copy-done) | data formatting | bytes 524288
Async XLA Ops:
  54.3 2.3 %copy-start.2 = (bf16[512,256]{1,0:T(8,128)(2,1)S(1)}, bf16[512,256]{1,0:T(8,128)(2,1)}, u32[]{:S(2)}) copy-start(bf16[512,256]{1,0:T(8,128)(2,1)} %get-tuple-element.9) | copy-start | bytes 786436
  56.6 1.0 %copy-start.1 = (bf16[512,256]{1,0:T(8,128)(2,1)S(1)}, bf16[512,256]{1,0:T(8,128)(2,1)}, u32[]{:S(2)}) copy-start(bf16[512,256]{1,0:T(8,128)(2,1)} %get-tuple-element.10) | copy-start | bytes 786436
  57.7 1.0 %copy-start = (bf16[512,256]{1,0:T(8,128)(2,1)S(1)}, bf16[512,256]{1,0:T(8,128)(2,1)}, u32[]{:S(2)}) copy-start(bf16[512,256]{1,0:T(8,128)(2,1)} %get-tuple-element.11) | copy-start | bytes 786436
